TPU v7x, 32 devices: a whole 2x2x4 slice. The times are simulated.
32 devices in a mesh: parts: 2 (over y), tm: 4 (over z), factor: 4 (over x, core).
Axes of the slice: x: 2, y: 2, z: 4, core: 2. Of those that a mesh axis runs over, the one named last changes fastest.
Arguments:
- schur_matrix: float32 [24576, 24, 4, 128], P(('parts', 'tm'), None, 'factor'), parts along dimension 0, as said below
- link_rhs: float32 [24576], P(('parts', 'tm')), parts along dimension 0, may hold values from -6 to 6
- hour_rhs: float32 [32, 256], P(('parts', 'tm', 'factor')), parts along dimension 0, may hold values from -6 to 6
- link_cols: int32 [32, 256], P(('parts', 'tm', 'factor')), parts along dimension 0, may hold values from 0 to 255
- link_coef: float32 [32, 256], P(('parts', 'tm', 'factor')), parts along dimension 0, may hold values from -6 to 6
- hour_inverse: float32 [32, 256, 256], P(('parts', 'tm', 'factor')), parts along dimension 0, may hold values from -0.375 to 0.375
- couple_prev: float32 [32, 2, 256], P(('parts', 'tm', 'factor')), parts along dimension 0, may hold values from -1.2 to 1.2
- couple_next: float32 [32, 2, 256], P(('parts', 'tm', 'factor')), parts along dimension 0, may hold values from -1.2 to 1.2
Outputs:
- schur_trail: float32 [24576, 24, 4, 128], P(('parts', 'tm'), None, 'factor'), parts along dimension 0
- link_trail: float32 [24576], P(('parts', 'tm')), parts along dimension 0
- hour_step: float32 [32, 256], P(('parts', 'tm', 'factor')), parts along dimension 0
There are 2 independent parts, one for each index of `parts`. A program takes and returns all parts, laid end to end along the dimension named above; each array names one. Nothing has to cross between parts.
Inputs may be any that keep to these rules, and one draw needn't show every extreme that they name: schur_matrix is symmetric and its leading 2 * 128 rows and columns form a positive definite block.
All inputs are finite; a program needn't handle non-finite values.
Results may differ from a plain program's by a relative error of at most 0.0001.
Values sent between devices are 32-bit elements; how exact they have to be, the bound alone decides.
A program may use at most 192 MiB of HBM per device.

v0:
```python
import jax
import jax.numpy as jnp
from jax import lax
from jax.sharding import PartitionSpec as P

PANELS = 2
BW = 2
SWEEPS = 2


def spread(array, axis, root):
    mine = lax.axis_index(axis) == root
    return lax.psum(jnp.where(mine, array, jnp.zeros_like(array)), axis)


def with_halo(cells, sides, width):
    for axis, dim in sides:
        count = lax.axis_size(axis)
        ends = count - 1
        head = lax.slice_in_dim(cells, 0, width, axis=dim)
        tail = lax.slice_in_dim(cells, cells.shape[dim] - width, cells.shape[dim], axis=dim)
        cells = jnp.concatenate(
            [
                lax.ppermute(tail, axis, [(i, (i + 1) % count) for i in range(ends)]),
                cells,
                lax.ppermute(head, axis, [((i + 1) % count, i) for i in range(ends)]),
            ],
            axis=dim,
        )
    return cells


def shards(
    schur_matrix, link_rhs, hour_rhs, link_cols, link_coef, hour_inverse, couple_prev, couple_next
):
    rows_here = schur_matrix.shape[0]
    tiles_here = schur_matrix.shape[1]
    width = schur_matrix.shape[3]
    factors = lax.axis_size("factor")
    row_start = lax.axis_index("tm") * rows_here
    global_rows = row_start + jnp.arange(rows_here, dtype=jnp.int32)
    factor_here = lax.axis_index("factor")
    schur_now = schur_matrix
    rhs_now = link_rhs
    solved = []
    for panel_id in range(PANELS):
        column_tile = panel_id // factors
        owner_index = panel_id % factors
        own_cols = schur_now[:, column_tile, 0, :]
        panel_cols = spread(own_cols, "factor", owner_index)
        panel_first = panel_id * width
        picker = (
            global_rows[:, None] - panel_first == jnp.arange(width, dtype=jnp.int32)[None, :]
        ).astype(jnp.float32)
        block_part = jnp.dot(picker.T, panel_cols, precision=lax.Precision.HIGHEST)
        rhs_part = jnp.dot(picker.T, rhs_now, precision=lax.Precision.HIGHEST)
        diag_block, rhs_segment = lax.psum((block_part, rhs_part), "tm")
        lower_block = jnp.linalg.cholesky(diag_block)
        factor_rows = jax.scipy.linalg.solve_triangular(lower_block, panel_cols.T, lower=True).T
        factor_rows = jnp.where(
            (global_rows < panel_first)[:, None], jnp.zeros_like(factor_rows), factor_rows
        )
        all_factor = lax.all_gather(factor_rows, "tm", axis=0, tiled=True)
        grouped = all_factor.reshape(tiles_here, factors, width, width)
        my_tiles = lax.dynamic_index_in_dim(grouped, factor_here, 1, keepdims=False)
        link_step = jax.scipy.linalg.solve_triangular(lower_block, rhs_segment, lower=True)
        rhs_now = rhs_now - jnp.dot(factor_rows, link_step, precision=lax.Precision.HIGHEST)
        update = jnp.einsum("rk,tck->rtc", factor_rows, my_tiles, precision=lax.Precision.HIGHEST)
        schur_now = schur_now - update[:, :, None, :]
        solved.append(link_step)
    link_values = jnp.concatenate(solved)
    one_hot = (
        link_cols[:, :, None] == jnp.arange(PANELS * width, dtype=jnp.int32)[None, None, :]
    ).astype(jnp.float32)
    looked = jnp.einsum("hik,k->hi", one_hot, link_values, precision=lax.Precision.HIGHEST)
    target = hour_rhs - link_coef * looked
    hour_state = jnp.einsum("hik,hk->hi", hour_inverse, target, precision=lax.Precision.HIGHEST)
    for sweep_id in range(SWEEPS):
        border_pairs = jnp.concatenate((hour_state[:, :BW], hour_state[:, -BW:]), axis=1)
        padded = with_halo(border_pairs, ((("tm", "factor"), 0),), 1)
        prev_last = padded[:-2, BW:]
        next_first = padded[2:, :BW]
        coupling = jnp.einsum("hbi,hb->hi", couple_prev, prev_last, precision=lax.Precision.HIGHEST)
        coupling = coupling + jnp.einsum(
            "hbi,hb->hi", couple_next, next_first, precision=lax.Precision.HIGHEST
        )
        hour_state = jnp.einsum(
            "hik,hk->hi", hour_inverse, target - coupling, precision=lax.Precision.HIGHEST
        )
    return (schur_now, rhs_now, hour_state)


def solution(mesh):
    placed = (
        P(("parts", "tm"), None, "factor", None),
        P(("parts", "tm")),
        P(("parts", "tm", "factor"), None),
        P(("parts", "tm", "factor"), None),
        P(("parts", "tm", "factor"), None),
        P(("parts", "tm", "factor"), None, None),
        P(("parts", "tm", "factor"), None, None),
        P(("parts", "tm", "factor"), None, None),
    )
    return jax.shard_map(
        shards,
        mesh=mesh,
        in_specs=placed,
        out_specs=(
            P(("parts", "tm"), None, "factor", None),
            P(("parts", "tm")),
            P(("parts", "tm", "factor"), None),
        ),
        check_vma=False,
    )
```

profile of v0, /device:TPU:0, one launch (start us, length us, event | category | flops | bytes accessed | tf_op | source)
XLA Modules:
  0.0 661.5 jit_solution(964721345408237185)
XLA Ops:
  7.2 32.9 %copy.16 = f32[3072,24,1,128]{3,0,1,2:T(8,128)} copy(f32[3072,24,1,128]{3,2,1,0:T(1,128)} %param.13) | data formatting | bytes 75497472 | tf_op args[0]
  40.2 2.7 fusion.1
  42.9 45.6 %all-reduce.5.cloned.1.call-done = f32[3072,128]{1,0:T(8,128)} async-done(((f32[3072,128]{1,0:T(8,128)}), f32[3072,128]{1,0:T(8,128)}) %all-reduce.5.cloned.1.call-update) | async-done | bytes 1572880 | tf_op jit(solution)/shard_map/psum | solution.py:13
  88.6 4.0 fusion.8
  92.6 34.1 %all-reduce.7.cloned.1.call-done = f32[128,128]{0,1:T(8,128)} async-done(((f32[128,128]{0,1:T(8,128)}), f32[128,128]{0,1:T(8,128)}) %all-reduce.7.cloned.1.call-update) | async-done | bytes 65552 | tf_op jit(solution)/shard_map/psum | solution.py:57
  128.6 11.7 %cholesky.44 = f32[128,128]{1,0:T(8,128)S(1)} custom-call(f32[128,128]{1,0:T(8,128)S(1)} %fusion.35), custom_call_target="Cholesky" | custom-call | tf_op jit(solution)/shard_map/jit(cholesky)/cholesky | solution.py:58
  141.6 9.8 %custom-call.10 = f32[1,128,128]{1,2,0:T(8,128)S(1)} custom-call(f32[1,128,128]{2,1,0:T(8,128)S(1)} %fusion.26), custom_call_target="InvertDiagBlocksLowerTriangular" | custom-call | tf_op jit(solution)/shard_map/jit(_solve_triangular)/triangular_solve | solution.py:59
  151.5 2.7 convolution_select_fusion.1
  154.7 114.7 %all-gather.3.cloned.1.call-done = f32[12288,128]{0,1:T(8,128)} async-done(((f32[3072,128]{0,1:T(8,128)}), f32[12288,128]{0,1:T(8,128)}) %all-gather.3.cloned.1.call-update) | async-done | bytes 6291472 | tf_op jit(solution)/shard_map/all_gather | solution.py:63
  269.3 8.3 %reshape.109 = f32[24,4,128,128]{2,1,0,3:T(4,128)} reshape(f32[12288,128]{0,1:T(8,128)} %all-gather.3.cloned.1.call-done) | data formatting | bytes 12582912 | tf_op jit(solution)/shard_map/reshape | solution.py:64
  277.7 5.6 constant_dynamic-slice_fusion.1
  283.2 3.8 copy.14
  287.1 41.2 %bitcast_subtract_fusion.1 = f32[3072,24,1,128]{3,0,1,2:T(8,128)} fusion(f32[24,1,128,128]{3,2,0,1:T(8,128)S(1)} %copy.14, f32[128,3072]{1,0:T(8,128)S(1)} %copy-done.3, f32[3072,24,1,128]{3,2,1,0:T(1,128)} %param.13), kind=kOutput, calls=%fused_computation.1 | convolution fusion | flops 14504951808 | bytes 78643200 | tf_op jit(solution)/shard_map/rk,tck->rtc/dot_general | solution.py:68
  328.3 2.7 fusion
  331.1 41.1 %all-reduce.9.cloned.1.call-done = f32[3072,128]{1,0:T(8,128)} async-done(((f32[3072,128]{1,0:T(8,128)}), f32[3072,128]{1,0:T(8,128)}) %all-reduce.9.cloned.1.call-update) | async-done | bytes 1572880 | tf_op jit(solution)/shard_map/psum | solution.py:13
  372.2 4.0 fusion.9
  376.5 34.0 %all-reduce.11.cloned.1.call-done = f32[128,128]{0,1:T(8,128)} async-done(((f32[128,128]{0,1:T(8,128)}), f32[128,128]{0,1:T(8,128)}) %all-reduce.11.cloned.1.call-update) | async-done | bytes 65552 | tf_op jit(solution)/shard_map/psum | solution.py:57
  412.9 12.5 %cholesky.55 = f32[128,128]{1,0:T(8,128)S(1)} custom-call(f32[128,128]{1,0:T(8,128)} %fusion.31), custom_call_target="Cholesky" | custom-call | tf_op jit(solution)/shard_map/jit(cholesky)/cholesky | solution.py:58
  427.4 10.6 %custom-call.11 = f32[1,128,128]{1,2,0:T(8,128)S(1)} custom-call(f32[1,128,128]{2,1,0:T(8,128)} %fusion.27), custom_call_target="InvertDiagBlocksLowerTriangular" | custom-call | tf_op jit(solution)/shard_map/jit(_solve_triangular)/triangular_solve | solution.py:59
  438.0 2.7 convolution_select_fusion
  440.7 2.1 fusion.14
  442.9 10.7 %psum.46 = f32[128]{0:T(128)S(1)} all-reduce(f32[128]{0:T(128)} %fusion.14), channel_id=1, replica_groups=mesh['parts'=2,'tm'=4,'factor'=4] {'tm'}, use_global_device_ids=true, to_apply=%region_6.9 | all-reduce | flops 128 | bytes 1024 | tf_op jit(solution)/shard_map/psum | solution.py:57
  455.4 1.5 fusion.13
  456.9 8.7 %psum.47 = f32[128]{0:T(128)S(1)} all-reduce(f32[128]{0:T(128)S(1)} %fusion.13), channel_id=1, replica_groups=mesh['parts'=2,'tm'=4,'factor'=4] {'tm'}, use_global_device_ids=true, to_apply=%region_7.11 | all-reduce | flops 128 | bytes 1024 | tf_op jit(solution)/shard_map/psum | solution.py:57
  468.6 3.0 collective-permute-start
  475.3 3.9 collective-permute-start.2
  480.9 75.3 %all-gather.5.cloned.1.call-done = f32[12288,128]{0,1:T(8,128)} async-done(((f32[3072,128]{0,1:T(8,128)}), f32[12288,128]{0,1:T(8,128)}) %all-gather.5.cloned.1.call-update) | async-done | bytes 6291472 | tf_op jit(solution)/shard_map/all_gather | solution.py:63
  556.2 8.3 %reshape.110 = f32[24,4,128,128]{2,1,0,3:T(4,128)} reshape(f32[12288,128]{0,1:T(8,128)} %all-gather.5.cloned.1.call-done) | data formatting | bytes 12582912 | tf_op jit(solution)/shard_map/reshape | solution.py:64
  564.5 5.6 constant_dynamic-slice_fusion
  570.1 3.7 copy.19
  573.8 37.3 %bitcast_subtract_fusion = f32[3072,24,1,128]{3,0,1,2:T(8,128)} fusion(f32[3072,24,1,128]{3,0,1,2:T(8,128)} %bitcast_subtract_fusion.1, f32[24,1,128,128]{3,2,0,1:T(8,128)S(1)} %copy.19, f32[128,3072]{1,0:T(8,128)S(1)} %copy-done.2), kind=kOutput, calls=%fused_computation | convolution fusion | flops 14504951808 | bytes 78643200 | tf_op jit(solution)/shard_map/rk,tck->rtc/dot_general | solution.py:68
  611.1 43.3 %copy.21 = f32[3072,24,1,128]{3,2,1,0:T(1,128)} copy(f32[3072,24,1,128]{3,0,1,2:T(8,128)} %bitcast_subtract_fusion) | data formatting | bytes 75497472
  (73 shorter events, 18.6 us)
Async XLA Ops:
  7.2 459.6 %copy-start = (f32[1,256,256]{2,1,0:T(8,128)S(1)}, f32[1,256,256]{2,1,0:T(8,128)}, u32[]{:S(2)}) copy-start(f32[1,256,256]{2,1,0:T(8,128)} %param.18) | copy-start | bytes 786436
  7.2 81.4 %all-reduce.5.cloned.1.call-start = ((), (), s32[]{:S(2)}) async-start(), calls=%async_computation | async-start | bytes 3145728 | tf_op jit(solution)/shard_map/psum | solution.py:13
  42.9 83.9 %all-reduce.7.cloned.1.call-start = ((), (), s32[]{:S(2)}) async-start(), calls=%async_computation.1 | async-start | bytes 131072 | tf_op jit(solution)/shard_map/psum | solution.py:57
  88.6 62.9 %copy-start.4 = (f32[3072,128]{1,0:T(8,128)S(1)}, f32[3072,128]{1,0:T(8,128)}, u32[]{:S(2)}) copy-start(f32[3072,128]{1,0:T(8,128)} %all-reduce.5.cloned.1.call-done) | copy-start | bytes 4718596
  92.6 176.8 %all-gather.3.cloned.1.call-start = ((), (), s32[]{:S(2)}) async-start(), calls=%async_computation.2 | async-start | bytes 7864320 | tf_op jit(solution)/shard_map/all_gather | solution.py:63
  154.1 218.1 %all-reduce.9.cloned.1.call-start = ((), (), s32[]{:S(2)}) async-start(), calls=%async_computation.3 | async-start | bytes 3145728 | tf_op jit(solution)/shard_map/psum | solution.py:13
  283.2 3.9 copy-start.3
  331.0 79.4 %all-reduce.11.cloned.1.call-start = ((), (), s32[]{:S(2)}) async-start(), calls=%async_computation.4 | async-start | bytes 131072 | tf_op jit(solution)/shard_map/psum | solution.py:57
  331.1 45.4 %copy-start.6 = (s32[3072]{0:T(1024)}, s32[3072]{0:T(1024)S(1)}, u32[]{:S(2)}) copy-start(s32[3072]{0:T(1024)S(1)} %fusion.36) | copy-start | bytes 36868
  372.2 65.8 %copy-start.5 = (f32[3072,128]{1,0:T(8,128)S(1)}, f32[3072,128]{1,0:T(8,128)}, u32[]{:S(2)}) copy-start(f32[3072,128]{1,0:T(8,128)} %all-reduce.9.cloned.1.call-done) | copy-start | bytes 4718596
  376.2 180.0 %all-gather.5.cloned.1.call-start = ((), (), s32[]{:S(2)}) async-start(), calls=%async_computation.5 | async-start | bytes 7864320 | tf_op jit(solution)/shard_map/all_gather | solution.py:63
  440.7 25.0 %copy-start.9 = (f32[1,256]{1,0:T(1,128)S(1)}, f32[1,256]{1,0:T(1,128)}, u32[]{:S(2)}) copy-start(f32[1,256]{1,0:T(1,128)} %param.15) | copy-start | bytes 3076
  440.7 30.9 %copy-start.2 = (f32[128,3072]{1,0:T(8,128)S(1)}, f32[128,3072]{1,0:T(8,128)}, u32[]{:S(2)}) copy-start(f32[128,3072]{1,0:T(8,128)} %convolution_select_fusion) | copy-start | bytes 4718596
  454.7 18.5 %copy-start.7 = (f32[1,2,256]{2,1,0:T(2,128)S(1)}, f32[1,2,256]{2,1,0:T(2,128)}, u32[]{:S(2)}) copy-start(f32[1,2,256]{2,1,0:T(2,128)} %param.20) | copy-start | bytes 6148
  454.7 18.6 %copy-start.8 = (f32[1,2,256]{2,1,0:T(2,128)S(1)}, f32[1,2,256]{2,1,0:T(2,128)}, u32[]{:S(2)}) copy-start(f32[1,2,256]{2,1,0:T(2,128)} %param.19) | copy-start | bytes 6148
  467.3 5.9 collective-permute-start.1
  468.6 4.7 collective-permute-start
  474.0 5.2 collective-permute-start.3
  475.3 4.5 collective-permute-start.2
  611.1 43.3 %copy-start.1 = (f32[1,256,256]{2,1,0:T(8,128)S(1)}, f32[1,256,256]{2,1,0:T(8,128)}, u32[]{:S(2)}) copy-start(f32[1,256,256]{2,1,0:T(8,128)} %param.18) | copy-start | bytes 786436
Sparse Core Ops, SparseCore 0:
  43.0 45.5 all-reduce.4
  92.7 34.0 all-reduce.6
  154.3 115.0 all-gather.2
  331.1 41.0 all-reduce.8
  376.4 34.0 all-reduce.10
  440.8 115.3 all-gather.4
where the time goes:
time: 671 us; the launch traced here: 662 us
  waiting for transfers between devices  345 us (51%)
  local copies, waits for them, and re-layouts  114 us (17%)
  matrix products  101 us (15%)
  other arithmetic  57.2 us (9%)
  blocking collectives  19.4 us (3%)
  between operations  14.7 us (2%)
  starting transfers between devices  10.4 us (2%)
    all_gather x2, waiting for transfers between devices, shards(): all_factor = lax.all_gather(factor_rows, 'tm', axis=0, tiled=True)  190 us
    psum x2, waiting for transfers between devices, spread(): return lax.psum(jnp.where(mine, array, jnp.zeros_like(array)), axis)  86.8 us
    dot_general x2, matrix products, shards(): jnp.einsum('rk,tck->rtc', factor_rows, my_tiles, precision=lax.Precision....  78.5 us
    unnamed x22, local copies, waits for them, and re-layouts  76.3 us
    psum x2, waiting for transfers between devices, shards(): diag_block, rhs_segment = lax.psum((block_part, rhs_part), 'tm')  68.1 us
    another operation x6, other arithmetic, shards(): lower_block = jnp.linalg.cholesky(diag_block)  25.6 us
    another operation x4, other arithmetic, shards(): jax.scipy.linalg.solve_triangular(lower_block, panel_cols.T, lower=True)  22.4 us
    psum x2, blocking collectives, shards(): diag_block, rhs_segment = lax.psum((block_part, rhs_part), 'tm')  19.4 us
  transfers between devices with their start and end apart: 10, of which 7 were waited for; matrix products, arithmetic and copies ran while one was open for 2% of the time, Pallas kernels for 0%

commit v1 on v0

--- a/solution.py
+++ b/solution.py
@@ -60,7 +60,14 @@
         factor_rows = jnp.where(
             (global_rows < panel_first)[:, None], jnp.zeros_like(factor_rows), factor_rows
         )
-        all_factor = lax.all_gather(factor_rows, "tm", axis=0, tiled=True)
+        ways, here = (lax.axis_size("tm"), lax.axis_index("tm"))
+        all_factor, reach = (factor_rows, 1)
+        while reach < ways:
+            theirs = lax.ppermute(all_factor, "tm", [(d, d ^ reach) for d in range(ways)])
+            mine_first = jnp.concatenate([all_factor, theirs], axis=0)
+            theirs_first = jnp.concatenate([theirs, all_factor], axis=0)
+            all_factor = jnp.where(here & reach == 0, mine_first, theirs_first)
+            reach = 2 * reach
         grouped = all_factor.reshape(tiles_here, factors, width, width)
         my_tiles = lax.dynamic_index_in_dim(grouped, factor_here, 1, keepdims=False)
         link_step = jax.scipy.linalg.solve_triangular(lower_block, rhs_segment, lower=True)

time: 671 us -> 819 us (1.22)
  the two profiles are of different devices: /device:TPU:0 before, /device:TPU:16 now
where the time goes in v1:
time: 819 us; the launch traced here: 814 us
  waiting for transfers between devices  328 us (40%)
  blocking collectives  170 us (21%)
  local copies, waits for them, and re-layouts  114 us (14%)
  matrix products  97 us (12%)
  other arithmetic  76.6 us (9%)
  starting transfers between devices  14.5 us (2%)
  between operations  14.3 us (2%)
    psum x2, blocking collectives, shards(): diag_block, rhs_segment = lax.psum((block_part, rhs_part), 'tm')  170 us
    ppermute x4, waiting for transfers between devices, shards(): lax.ppermute(all_factor, 'tm', [(d, d ^ reach) for d in range(ways)])  166 us
    psum x2, waiting for transfers between devices, spread(): return lax.psum(jnp.where(mine, array, jnp.zeros_like(array)), axis)  89.6 us
    dot_general x2, matrix products, shards(): jnp.einsum('rk,tck->rtc', factor_rows, my_tiles, precision=lax.Precision....  78.5 us
    unnamed x24, local copies, waits for them, and re-layouts  76.3 us
    psum x2, waiting for transfers between devices, shards(): diag_block, rhs_segment = lax.psum((block_part, rhs_part), 'tm')  67.5 us
    another operation x6, other arithmetic, shards(): lower_block = jnp.linalg.cholesky(diag_block)  24.8 us
    select_n x4, other arithmetic, shards(): all_factor = jnp.where(here & reach == 0, mine_first, theirs_first)  22.3 us
  transfers between devices with their start and end apart: 12, of which 8 were waited for; matrix products, arithmetic and copies ran while one was open for 1% of the time, Pallas kernels for 0%

profile of v1, /device:TPU:16, one launch (start us, length us, event | category | flops | bytes accessed | tf_op | source)
XLA Modules:
  0.0 814.3 jit_solution(361373015431380275)
XLA Ops:
  7.2 32.9 %copy.16 = f32[3072,24,1,128]{3,0,1,2:T(8,128)} copy(f32[3072,24,1,128]{3,2,1,0:T(1,128)} %param.13) | data formatting | bytes 75497472 | tf_op args[0]
  40.2 2.7 fusion.1
  42.9 44.0 %all-reduce.5.cloned.1.call-done = f32[3072,128]{1,0:T(8,128)} async-done(((f32[3072,128]{1,0:T(8,128)}), f32[3072,128]{1,0:T(8,128)}) %all-reduce.5.cloned.1.call-update) | async-done | bytes 1572880 | tf_op jit(solution)/shard_map/psum | solution.py:13
  86.9 4.0 fusion.8
  91.3 33.6 %all-reduce.7.cloned.1.call-done = f32[128,128]{0,1:T(8,128)} async-done(((f32[128,128]{0,1:T(8,128)}), f32[128,128]{0,1:T(8,128)}) %all-reduce.7.cloned.1.call-update) | async-done | bytes 65552 | tf_op jit(solution)/shard_map/psum | solution.py:57
  126.7 11.7 %cholesky.44 = f32[128,128]{1,0:T(8,128)S(1)} custom-call(f32[128,128]{1,0:T(8,128)S(1)} %fusion.35), custom_call_target="Cholesky" | custom-call | tf_op jit(solution)/shard_map/jit(cholesky)/cholesky | solution.py:58
  139.7 9.8 %custom-call.10 = f32[1,128,128]{1,2,0:T(8,128)S(1)} custom-call(f32[1,128,128]{2,1,0:T(8,128)S(1)} %fusion.26), custom_call_target="InvertDiagBlocksLowerTriangular" | custom-call | tf_op jit(solution)/shard_map/jit(_solve_triangular)/triangular_solve | solution.py:59
  151.7 33.7 %collective-permute-done = f32[3072,128]{0,1:T(8,128)S(1)} collective-permute-done((f32[3072,128]{0,1:T(8,128)S(1)}, f32[3072,128]{0,1:T(8,128)S(1)}, u32[]{:S(2)}, u32[]{:S(2)}) %collective-permute-start) | collective-permute-done | bytes 1572896 | tf_op jit(solution)/shard_map/ppermute | solution.py:66
  188.1 132.2 %collective-permute-done.1 = f32[6144,128]{0,1:T(8,128)} collective-permute-done((f32[6144,128]{0,1:T(8,128)}, f32[6144,128]{0,1:T(8,128)}, u32[]{:S(2)}, u32[]{:S(2)}) %collective-permute-start.1) | collective-permute-done | bytes 3145760 | tf_op jit(solution)/shard_map/ppermute | solution.py:66
  320.3 8.5 %maximum_select_fusion = f32[12288,128]{0,1:T(8,128)} fusion(f32[6144,128]{0,1:T(8,128)} %collective-permute-done.1, f32[6144,128]{0,1:T(8,128)} %maximum_select_fusion.2, pred[]{:T(512)S(6)} %eq.76), kind=kLoop, calls=%fused_computation.2 | loop fusion | flops 4718592 | bytes 12582913 | tf_op jit(solution)/shard_map/jit(_where)/select_n | solution.py:69
  328.8 8.3 %select_n.82 = f32[24,4,128,128]{2,1,0,3:T(4,128)} reshape(f32[12288,128]{0,1:T(8,128)} %maximum_select_fusion) | data formatting | bytes 12582912 | tf_op jit(solution)/shard_map/jit(_where)/select_n | solution.py:69
  337.1 5.5 constant_dynamic-slice_fusion.1
  342.7 3.7 copy.14
  346.4 41.2 %bitcast_subtract_fusion.1 = f32[3072,24,1,128]{3,0,1,2:T(8,128)} fusion(f32[24,1,128,128]{3,2,0,1:T(8,128)S(1)} %copy.14, f32[128,3072]{1,0:T(8,128)S(1)} %convolution_select_fusion.1, f32[3072,24,1,128]{3,2,1,0:T(1,128)} %param.13), kind=kOutput, calls=%fused_computation.1 | convolution fusion | flops 14504951808 | bytes 78643200 | tf_op jit(solution)/shard_map/rk,tck->rtc/dot_general | solution.py:75
  387.6 2.7 fusion
  390.6 45.6 %all-reduce.9.cloned.1.call-done = f32[3072,128]{1,0:T(8,128)} async-done(((f32[3072,128]{1,0:T(8,128)}), f32[3072,128]{1,0:T(8,128)}) %all-reduce.9.cloned.1.call-update) | async-done | bytes 1572880 | tf_op jit(solution)/shard_map/psum | solution.py:13
  436.2 3.9 fusion.9
  440.1 33.9 %all-reduce.11.cloned.1.call-done = f32[128,128]{0,1:T(8,128)} async-done(((f32[128,128]{0,1:T(8,128)}), f32[128,128]{0,1:T(8,128)}) %all-reduce.11.cloned.1.call-update) | async-done | bytes 65552 | tf_op jit(solution)/shard_map/psum | solution.py:57
  475.8 11.7 %cholesky.55 = f32[128,128]{1,0:T(8,128)S(1)} custom-call(f32[128,128]{1,0:T(8,128)S(1)} %fusion.31), custom_call_target="Cholesky" | custom-call | tf_op jit(solution)/shard_map/jit(cholesky)/cholesky | solution.py:58
  488.8 9.8 %custom-call.11 = f32[1,128,128]{1,2,0:T(8,128)S(1)} custom-call(f32[1,128,128]{2,1,0:T(8,128)S(1)} %fusion.27), custom_call_target="InvertDiagBlocksLowerTriangular" | custom-call | tf_op jit(solution)/shard_map/jit(_solve_triangular)/triangular_solve | solution.py:59
  498.7 2.9 convolution_select_fusion
  503.0 35.4 %psum.46 = f32[128]{0:T(128)S(1)} all-reduce(f32[128]{0:T(128)S(1)} %fusion.14), channel_id=1, replica_groups=mesh['parts'=2,'tm'=4,'factor'=4] {'tm'}, use_global_device_ids=true, to_apply=%region_6.9 | all-reduce | flops 128 | bytes 1024 | tf_op jit(solution)/shard_map/psum | solution.py:57
  540.2 3.9 maximum_select_fusion.3
  544.2 3.2 collective-permute-start.3
  548.2 134.5 %psum.47 = f32[128]{0:T(128)S(1)} all-reduce(f32[128]{0:T(128)S(1)} %fusion.13), channel_id=1, replica_groups=mesh['parts'=2,'tm'=4,'factor'=4] {'tm'}, use_global_device_ids=true, to_apply=%region_7.11 | all-reduce | flops 128 | bytes 1024 | tf_op jit(solution)/shard_map/psum | solution.py:57
  696.6 3.7 collective-permute-done.6
  701.4 7.9 maximum_select_fusion.1
  709.3 8.3 %select_n.91 = f32[24,4,128,128]{2,1,0,3:T(4,128)} reshape(f32[12288,128]{0,1:T(8,128)} %maximum_select_fusion.1) | data formatting | bytes 12582912 | tf_op jit(solution)/shard_map/jit(_where)/select_n | solution.py:69
  717.6 5.6 constant_dynamic-slice_fusion
  723.1 3.7 copy.19
  726.9 37.3 %bitcast_subtract_fusion = f32[3072,24,1,128]{3,0,1,2:T(8,128)} fusion(f32[3072,24,1,128]{3,0,1,2:T(8,128)} %bitcast_subtract_fusion.1, f32[24,1,128,128]{3,2,0,1:T(8,128)S(1)} %copy.19, f32[128,3072]{1,0:T(8,128)S(1)} %convolution_select_fusion), kind=kOutput, calls=%fused_computation | convolution fusion | flops 14504951808 | bytes 78643200 | tf_op jit(solution)/shard_map/rk,tck->rtc/dot_general | solution.py:75
  764.2 43.3 %copy.21 = f32[3072,24,1,128]{3,2,1,0:T(1,128)} copy(f32[3072,24,1,128]{3,0,1,2:T(8,128)} %bitcast_subtract_fusion) | data formatting | bytes 75497472
  (81 shorter events, 30.7 us)
Async XLA Ops:
  7.2 676.1 %copy-start = (f32[1,256,256]{2,1,0:T(8,128)S(1)}, f32[1,256,256]{2,1,0:T(8,128)}, u32[]{:S(2)}) copy-start(f32[1,256,256]{2,1,0:T(8,128)} %param.18) | copy-start | bytes 786436
  7.2 79.7 %all-reduce.5.cloned.1.call-start = ((), (), s32[]{:S(2)}) async-start(), calls=%async_computation | async-start | bytes 3145728 | tf_op jit(solution)/shard_map/psum | solution.py:13
  42.9 82.0 %all-reduce.7.cloned.1.call-start = ((), (), s32[]{:S(2)}) async-start(), calls=%async_computation.1 | async-start | bytes 131072 | tf_op jit(solution)/shard_map/psum | solution.py:57
  86.9 62.6 %copy-start.2 = (f32[3072,128]{1,0:T(8,128)S(1)}, f32[3072,128]{1,0:T(8,128)}, u32[]{:S(2)}) copy-start(f32[3072,128]{1,0:T(8,128)} %all-reduce.5.cloned.1.call-done) | copy-start | bytes 4718596
  91.0 345.2 %all-reduce.9.cloned.1.call-start = ((), (), s32[]{:S(2)}) async-start(), calls=%async_computation.2 | async-start | bytes 3145728 | tf_op jit(solution)/shard_map/psum | solution.py:13
  151.1 34.3 %collective-permute-start = (f32[3072,128]{0,1:T(8,128)S(1)}, f32[3072,128]{0,1:T(8,128)S(1)}, u32[]{:S(2)}, u32[]{:S(2)}) collective-permute-start(f32[3072,128]{0,1:T(8,128)S(1)} %bitcast.148), channel_id=1, source_target_pairs={{0,4},{4,0},{8,12},{12,8},{1,5},{5,1},{9,13},{13,9},{2,6},{6,2},{1... | collective-permute-start | bytes 4718600 | tf_op jit(solution)/shard_map/ppermute | solution.py:66
  187.3 132.9 %collective-permute-start.1 = (f32[6144,128]{0,1:T(8,128)}, f32[6144,128]{0,1:T(8,128)}, u32[]{:S(2)}, u32[]{:S(2)}) collective-permute-start(f32[6144,128]{0,1:T(8,128)} %maximum_select_fusion.2), channel_id=1, source_target_pairs={{0,8},{4,12},{8,0},{12,4},{1,9},{5,13},{9,1},{13,5},{2,10},{6,14},... | collective-permute-start | bytes 9437192 | tf_op jit(solution)/shard_map/ppermute | solution.py:66
  390.3 83.7 %all-reduce.11.cloned.1.call-start = ((), (), s32[]{:S(2)}) async-start(), calls=%async_computation.3 | async-start | bytes 131072 | tf_op jit(solution)/shard_map/psum | solution.py:57
  390.6 97.6 %copy-start.3 = (s32[3072]{0:T(1024)}, s32[3072]{0:T(1024)S(1)}, u32[]{:S(2)}) copy-start(s32[3072]{0:T(1024)S(1)} %fusion.36) | copy-start | bytes 36868
  498.7 3.6 copy-start.5
  501.6 38.6 %collective-permute-start.2 = (f32[3072,128]{0,1:T(8,128)S(1)}, f32[3072,128]{0,1:T(8,128)}, u32[]{:S(2)}, u32[]{:S(2)}) collective-permute-start(f32[3072,128]{0,1:T(8,128)S(1)} %bitcast.146), channel_id=1, source_target_pairs={{0,4},{4,0},{8,12},{12,8},{1,5},{5,1},{9,13},{13,9},{2,6},{6,2},{1... | collective-permute-start | bytes 4718600 | tf_op jit(solution)/shard_map/ppermute | solution.py:66
  540.2 7.2 copy-start.4
  540.2 142.7 %copy-start.8 = (f32[1,256]{1,0:T(1,128)S(1)}, f32[1,256]{1,0:T(1,128)}, u32[]{:S(2)}) copy-start(f32[1,256]{1,0:T(1,128)} %param.15) | copy-start | bytes 3076
  540.2 142.7 %copy-start.9 = (f32[1,256]{1,0:T(1,128)S(1)}, f32[1,256]{1,0:T(1,128)}, u32[]{:S(2)}) copy-start(f32[1,256]{1,0:T(1,128)} %param.17) | copy-start | bytes 3076
  540.2 142.7 %copy-start.10 = (s32[1,256]{1,0:T(1,128)S(1)}, s32[1,256]{1,0:T(1,128)}, u32[]{:S(2)}) copy-start(s32[1,256]{1,0:T(1,128)} %param.16) | copy-start | bytes 3076
  544.2 145.5 %copy-start.6 = (f32[1,2,256]{2,1,0:T(2,128)S(1)}, f32[1,2,256]{2,1,0:T(2,128)}, u32[]{:S(2)}) copy-start(f32[1,2,256]{2,1,0:T(2,128)} %param.20) | copy-start | bytes 6148
  544.2 147.3 %copy-start.7 = (f32[1,2,256]{2,1,0:T(2,128)S(1)}, f32[1,2,256]{2,1,0:T(2,128)}, u32[]{:S(2)}) copy-start(f32[1,2,256]{2,1,0:T(2,128)} %param.19) | copy-start | bytes 6148
  544.2 157.2 %collective-permute-start.3 = (f32[6144,128]{0,1:T(8,128)}, f32[6144,128]{0,1:T(8,128)}, u32[]{:S(2)}, u32[]{:S(2)}) collective-permute-start(f32[6144,128]{0,1:T(8,128)} %maximum_select_fusion.3), channel_id=1, source_target_pairs={{0,8},{4,12},{8,0},{12,4},{1,9},{5,13},{9,1},{13,5},{2,10},{6,14},... | collective-permute-start | bytes 9437192 | tf_op jit(solution)/shard_map/ppermute | solution.py:66
  683.8 5.9 collective-permute-start.5
  685.7 5.8 collective-permute-start.4
  692.1 4.3 collective-permute-start.7
  694.5 5.8 collective-permute-start.6
  764.2 43.3 %copy-start.1 = (f32[1,256,256]{2,1,0:T(8,128)S(1)}, f32[1,256,256]{2,1,0:T(8,128)}, u32[]{:S(2)}) copy-start(f32[1,256,256]{2,1,0:T(8,128)} %param.18) | copy-start | bytes 786436
Sparse Core Ops, SparseCore 0:
  43.0 43.9 all-reduce.4
  91.1 33.7 all-reduce.6
  390.4 45.7 all-reduce.8
  440.2 33.7 all-reduce.10
